TPU v7x, 32 devices: a whole 2x2x4 slice. The times are simulated.
32 devices in a mesh: seq: 2 (over y), rows: 16 (over z, x, core).
Axes of the slice: x: 2, y: 2, z: 4, core: 2. Of those that a mesh axis runs over, the one named last changes fastest.
Arguments:
- inputs: bfloat16 [32, 1024, 768], P('rows', 'seq'), may hold values from -6 to 6
- doc_ids: int32 [32, 1024], P('rows', 'seq'), may hold values from 0 to 1023, as said below
- first_gain: float32 [768], replicated, may hold values from 0.1 to 1.9
- first_shift: float32 [768], replicated, may hold values from -3 to 3
- qkv_weight: bfloat16 [768, 2304], replicated, may hold values from -0.21875 to 0.21875
- query_bias: float32 [768], replicated, may hold values from -2 to 2
- value_bias: float32 [768], replicated, may hold values from -2 to 2
- out_weight: bfloat16 [768, 768], replicated, may hold values from -3.5 to 3.5
- out_bias: float32 [768], replicated, may hold values from -3 to 3
- second_gain: float32 [768], replicated, may hold values from 0.1 to 1.9
- second_shift: float32 [768], replicated, may hold values from -3 to 3
- fc_weight: bfloat16 [768, 3072], replicated, may hold values from -0.21875 to 0.21875
- fc_bias: float32 [3072], replicated, may hold values from -2 to 2
- proj_weight: bfloat16 [3072, 768], replicated, may hold values from -0.625 to 0.625
- proj_bias: float32 [768], replicated, may hold values from -3 to 3
- cotangent: bfloat16 [32, 1024, 768], P('rows', 'seq'), may hold values from -6 to 6
Outputs:
- output: bfloat16 [32, 1024, 768], P('rows', 'seq')
- grad_inputs: bfloat16 [32, 1024, 768], P('rows', 'seq')
- grad_first_gain: float32 [768], P('rows')
- grad_first_shift: float32 [768], P('rows')
- grad_qkv_weight: float32 [768, 2304], P('rows')
- grad_query_bias: float32 [768], P('rows')
- grad_value_bias: float32 [768], P('rows')
- grad_out_weight: float32 [768, 768], P('rows')
- grad_out_bias: float32 [768], P('rows')
- grad_second_gain: float32 [768], P('rows')
- grad_second_shift: float32 [768], P('rows')
- grad_fc_weight: float32 [768, 3072], P('rows')
- grad_fc_bias: float32 [3072], P('rows')
- grad_proj_weight: float32 [3072, 768], P('rows')
- grad_proj_bias: float32 [768], P('rows')
Inputs may be any that keep to these rules, and one draw needn't show every extreme that they name: `doc_ids`: every document is a run of adjacent tokens of one row, and its tokens share one number that no other document of the row has; the numbers never fall along a row; the first document of every row has the number 0 and the last one 1024 - 1.
All inputs are finite; a program needn't handle non-finite values.
Results may differ from a plain program's by a relative error of at most 0.019.
Values may be sent and summed in bfloat16 or wider, within the bound.
A program may use at most 320 MiB of HBM per device.

v0:
```python
import jax
import jax.numpy as jnp
from jax import lax
from jax.sharding import PartitionSpec as P

H = 12
HD = 64
LAYERS = 12


epsilon = 1e-05
masked_value = -1e30


def layer_norm(values, norm_gain, norm_bias):
    row_mean = jnp.mean(values, axis=-1, keepdims=True)
    centred = values - row_mean
    variance = jnp.mean(centred * centred, axis=-1, keepdims=True)
    return centred * lax.rsqrt(variance + epsilon) * norm_gain + norm_bias


def gelu_tanh(values):
    return jax.nn.gelu(values, approximate=True)


def matmul_rows(left_side, weight):
    flat_rows = left_side.reshape(-1, left_side.shape[-1])
    result = jnp.dot(flat_rows, weight, preferred_element_type=jnp.float32)
    return result.reshape(left_side.shape[:-1] + (weight.shape[1],))


def back_rows(grads_low, weight):
    flat_rows = grads_low.reshape(-1, grads_low.shape[-1])
    result = jnp.einsum("nm,km->nk", flat_rows, weight, preferred_element_type=jnp.float32)
    return result.reshape(grads_low.shape[:-1] + (weight.shape[0],))


def weight_grad(left_side, right_side):
    left_flat = left_side.reshape(-1, left_side.shape[-1])
    right_flat = right_side.reshape(-1, right_side.shape[-1])
    return jnp.einsum("nk,nm->km", left_flat, right_flat, preferred_element_type=jnp.float32)


def column_sums(values):
    return jnp.sum(values.astype(jnp.float32), axis=(0, 1))


def visible(query_pos, query_doc, key_pos, key_doc):
    causal = key_pos[None, None, :] <= query_pos[None, :, None]
    same_doc = key_doc[:, None, :] == query_doc[:, :, None]
    return (causal & same_doc)[:, None]


def split_heads(kv_part):
    rows_here, key_count = (kv_part.shape[0], kv_part.shape[1])
    model_width = H * HD
    key_heads = kv_part[..., :model_width].reshape(rows_here, key_count, H, HD)
    return (key_heads, rows_here, key_count)


def scaled_scores(query_heads, key_heads, allowed):
    raw_scores = jnp.einsum(
        "rqhd,rkhd->rhqk", query_heads, key_heads, preferred_element_type=jnp.float32
    )
    return jnp.where(allowed, raw_scores * HD ** (-0.5), masked_value)


def guarded(folder, query_pos, query_doc):

    def update(totals, portion, offset):
        doc_part = portion[1]
        early_enough = offset <= query_pos[-1]
        doc_meets = jnp.any(jnp.max(doc_part, axis=1) >= jnp.min(query_doc, axis=1))
        return lax.cond(
            early_enough & doc_meets,
            lambda carried: folder(carried, portion, offset),
            lambda carried: carried,
            totals,
        )

    return update


def stats_update(query_heads, query_pos, query_doc):

    def update(totals, portion, offset):
        running_top, row_mass = totals
        kv_part, doc_part = portion
        key_heads, rows_here, key_count = split_heads(kv_part)
        key_pos = jnp.arange(key_count, dtype=jnp.int32)
        allowed = visible(query_pos, query_doc, key_pos, doc_part)
        scores = scaled_scores(query_heads, key_heads, allowed)
        new_top = jnp.maximum(running_top, jnp.max(scores, axis=-1))
        weights = jnp.where(allowed, jnp.exp(scores - new_top[..., None]), 0.0)
        row_mass = jnp.sum(weights, axis=-1)
        return (new_top, row_mass)

    return guarded(update, query_pos, query_doc)


def output_update(query_heads, query_pos, query_doc, running_top, row_mass):

    def update(totals, portion, offset):
        kv_part, doc_part = portion
        key_heads, rows_here, key_count = split_heads(kv_part)
        value_heads = kv_part[..., H * HD :].reshape(rows_here, key_count, H, HD)
        key_pos = jnp.arange(key_count, dtype=jnp.int32)
        allowed = visible(query_pos, query_doc, key_pos, doc_part)
        scores = scaled_scores(query_heads, key_heads, allowed)
        attn_probs = (
            jnp.where(allowed, jnp.exp(scores - running_top[..., None]), 0.0) / row_mass[..., None]
        )
        result = jnp.einsum(
            "rhqk,rkhd->rqhd",
            attn_probs.astype(jnp.bfloat16),
            value_heads,
            preferred_element_type=jnp.float32,
        )
        return result.reshape(totals.shape)

    return guarded(update, query_pos, query_doc)


def backward_update(
    query_heads, grad_heads, query_pos, query_doc, running_top, row_mass, row_delta
):

    def update(totals, portion, offset):
        grad_query, kv_grads = totals
        kv_part, doc_part = portion
        key_heads, rows_here, key_count = split_heads(kv_part)
        value_heads = kv_part[..., H * HD :].reshape(rows_here, key_count, H, HD)
        key_pos = jnp.arange(key_count, dtype=jnp.int32)
        allowed = visible(query_pos, query_doc, key_pos, doc_part)
        scores = scaled_scores(query_heads, key_heads, allowed)
        attn_probs = (
            jnp.where(allowed, jnp.exp(scores - running_top[..., None]), 0.0) / row_mass[..., None]
        )
        grad_probs = jnp.einsum(
            "rqhd,rkhd->rhqk", grad_heads, value_heads, preferred_element_type=jnp.float32
        )
        grad_scores = (attn_probs * (grad_probs - row_delta[..., None]) * HD ** (-0.5)).astype(
            jnp.bfloat16
        )
        query_part = jnp.einsum(
            "rhqk,rkhd->rqhd", grad_scores, key_heads, preferred_element_type=jnp.float32
        )
        grad_query = query_part.reshape(grad_query.shape)
        key_part = jnp.einsum(
            "rhqk,rqhd->rkhd", grad_scores, query_heads, preferred_element_type=jnp.float32
        )
        value_part = jnp.einsum(
            "rhqk,rqhd->rkhd",
            attn_probs.astype(jnp.bfloat16),
            grad_heads,
            preferred_element_type=jnp.float32,
        )
        piece_grads = jnp.concatenate(
            [
                key_part.reshape(rows_here, key_count, H * HD),
                value_part.reshape(rows_here, key_count, H * HD),
            ],
            axis=-1,
        )
        kv_grads = piece_grads
        return (grad_query, kv_grads)

    return guarded(update, query_pos, query_doc)


def local(
    inputs,
    doc_ids,
    first_gain,
    first_shift,
    qkv_weight,
    query_bias,
    value_bias,
    out_weight,
    out_bias,
    second_gain,
    second_shift,
    fc_weight,
    fc_bias,
    proj_weight,
    proj_bias,
    cotangent,
):
    branch_scale = LAYERS ** (-0.5)
    rows_here, tokens_here, model_width = inputs.shape
    seq_count = lax.axis_size("seq")
    seq_place = lax.axis_index("seq")
    query_pos = seq_place * tokens_here + jnp.arange(tokens_here, dtype=jnp.int32)
    residual = inputs.astype(jnp.float32)
    normed_first, first_pull = jax.vjp(layer_norm, residual, first_gain, first_shift)
    normed_first_low = normed_first.astype(jnp.bfloat16)
    bias_row = jnp.concatenate([query_bias, jnp.zeros_like(query_bias), value_bias])
    mixed_proj = (matmul_rows(normed_first_low, qkv_weight) + bias_row).astype(jnp.bfloat16)
    query_heads = mixed_proj[..., :model_width].reshape(rows_here, tokens_here, H, HD)
    key_values = mixed_proj[..., model_width:]
    init_top = jnp.full((rows_here, H, tokens_here), masked_value, jnp.float32)
    init_mass = jnp.zeros((rows_here, H, tokens_here), jnp.float32)
    stats_fold = stats_update(query_heads, query_pos, doc_ids)
    running_top, row_mass = stats_fold(
        (init_top, init_mass),
        (
            lax.all_gather(key_values[..., :model_width], "seq", axis=1, tiled=True),
            lax.all_gather(doc_ids, "seq", axis=1, tiled=True),
        ),
        jnp.int32(0),
    )
    out_fold = output_update(query_heads, query_pos, doc_ids, running_top, row_mass)
    zero_rows = jnp.zeros((rows_here, tokens_here, model_width), jnp.float32)
    attended = out_fold(
        zero_rows,
        (
            lax.all_gather(key_values, "seq", axis=1, tiled=True),
            lax.all_gather(doc_ids, "seq", axis=1, tiled=True),
        ),
        jnp.int32(0),
    )
    attended_low = attended.astype(jnp.bfloat16)
    branch_one = matmul_rows(attended_low, out_weight) + out_bias
    middle = residual + branch_scale * branch_one
    normed_second, second_pull = jax.vjp(layer_norm, middle, second_gain, second_shift)
    normed_second_low = normed_second.astype(jnp.bfloat16)
    hidden = matmul_rows(normed_second_low, fc_weight) + fc_bias
    activated, gelu_pull = jax.vjp(gelu_tanh, hidden)
    activated_low = activated.astype(jnp.bfloat16)
    branch_two = matmul_rows(activated_low, proj_weight) + proj_bias
    output = (middle + branch_scale * branch_two).astype(jnp.bfloat16)
    grad_output = cotangent.astype(jnp.float32)
    grad_branch_two = (branch_scale * grad_output).astype(jnp.bfloat16)
    grad_proj_weight = weight_grad(activated_low, grad_branch_two)
    grad_proj_bias = column_sums(grad_branch_two)
    grad_activated = back_rows(grad_branch_two, proj_weight)
    grad_hidden = gelu_pull(grad_activated)[0].astype(jnp.bfloat16)
    grad_fc_weight = weight_grad(normed_second_low, grad_hidden)
    grad_fc_bias = column_sums(grad_hidden)
    grad_normed_second = back_rows(grad_hidden, fc_weight)
    grad_from_norm, grad_second_gain, grad_second_shift = second_pull(grad_normed_second)
    grad_middle = grad_output + grad_from_norm
    grad_branch_one = (branch_scale * grad_middle).astype(jnp.bfloat16)
    grad_out_weight = weight_grad(attended_low, grad_branch_one)
    grad_out_bias = column_sums(grad_branch_one)
    grad_attended = back_rows(grad_branch_one, out_weight).astype(jnp.bfloat16)
    grad_heads = grad_attended.reshape(rows_here, tokens_here, H, HD)
    row_delta = jnp.einsum(
        "rqhd,rqhd->rhq",
        grad_heads.astype(jnp.float32),
        attended.reshape(rows_here, tokens_here, H, HD),
    )
    back_fold = backward_update(
        query_heads, grad_heads, query_pos, doc_ids, running_top, row_mass, row_delta
    )
    back_initial = (
        jnp.zeros((rows_here, tokens_here, model_width), jnp.float32),
        jnp.zeros((rows_here, tokens_here * seq_count, 2 * model_width), jnp.float32),
    )
    grad_query, kv_grads = back_fold(
        back_initial,
        (
            lax.all_gather(key_values, "seq", axis=1, tiled=True),
            lax.all_gather(doc_ids, "seq", axis=1, tiled=True),
        ),
        jnp.int32(0),
    )
    kv_summed = lax.psum_scatter(
        kv_grads.astype(jnp.bfloat16), "seq", scatter_dimension=1, tiled=True
    )
    grad_mixed = jnp.concatenate([grad_query.astype(jnp.bfloat16), kv_summed], axis=-1)
    grad_qkv_weight = weight_grad(normed_first_low, grad_mixed)
    mixed_sums = column_sums(grad_mixed)
    grad_query_bias = mixed_sums[:model_width]
    grad_value_bias = mixed_sums[2 * model_width :]
    grad_normed_first = back_rows(grad_mixed, qkv_weight)
    grad_from_first, grad_first_gain, grad_first_shift = first_pull(grad_normed_first)
    grad_inputs = (grad_middle + grad_from_first).astype(jnp.bfloat16)
    all_shares = (
        lax.psum_scatter(
            grad_first_gain.astype(jnp.bfloat16), "rows", scatter_dimension=0, tiled=True
        ).astype(jnp.float32),
        lax.psum_scatter(
            grad_first_shift.astype(jnp.bfloat16), "rows", scatter_dimension=0, tiled=True
        ).astype(jnp.float32),
        lax.psum_scatter(
            grad_qkv_weight.astype(jnp.bfloat16), "rows", scatter_dimension=0, tiled=True
        ).astype(jnp.float32),
        lax.psum_scatter(
            grad_query_bias.astype(jnp.bfloat16), "rows", scatter_dimension=0, tiled=True
        ).astype(jnp.float32),
        lax.psum_scatter(
            grad_value_bias.astype(jnp.bfloat16), "rows", scatter_dimension=0, tiled=True
        ).astype(jnp.float32),
        lax.psum_scatter(
            grad_out_weight.astype(jnp.bfloat16), "rows", scatter_dimension=0, tiled=True
        ).astype(jnp.float32),
        lax.psum_scatter(
            grad_out_bias.astype(jnp.bfloat16), "rows", scatter_dimension=0, tiled=True
        ).astype(jnp.float32),
        lax.psum_scatter(
            grad_second_gain.astype(jnp.bfloat16), "rows", scatter_dimension=0, tiled=True
        ).astype(jnp.float32),
        lax.psum_scatter(
            grad_second_shift.astype(jnp.bfloat16), "rows", scatter_dimension=0, tiled=True
        ).astype(jnp.float32),
        lax.psum_scatter(
            grad_fc_weight.astype(jnp.bfloat16), "rows", scatter_dimension=0, tiled=True
        ).astype(jnp.float32),
        lax.psum_scatter(
            grad_fc_bias.astype(jnp.bfloat16), "rows", scatter_dimension=0, tiled=True
        ).astype(jnp.float32),
        lax.psum_scatter(
            grad_proj_weight.astype(jnp.bfloat16), "rows", scatter_dimension=0, tiled=True
        ).astype(jnp.float32),
        lax.psum_scatter(
            grad_proj_bias.astype(jnp.bfloat16), "rows", scatter_dimension=0, tiled=True
        ).astype(jnp.float32),
    )
    (
        grad_first_gain,
        grad_first_shift,
        grad_qkv_weight,
        grad_query_bias,
        grad_value_bias,
        grad_out_weight,
        grad_out_bias,
        grad_second_gain,
        grad_second_shift,
        grad_fc_weight,
        grad_fc_bias,
        grad_proj_weight,
        grad_proj_bias,
    ) = (
        lax.psum(all_shares[0].astype(jnp.bfloat16), "seq").astype(jnp.float32),
        lax.psum(all_shares[1].astype(jnp.bfloat16), "seq").astype(jnp.float32),
        lax.psum(all_shares[2].astype(jnp.bfloat16), "seq").astype(jnp.float32),
        lax.psum(all_shares[3].astype(jnp.bfloat16), "seq").astype(jnp.float32),
        lax.psum(all_shares[4].astype(jnp.bfloat16), "seq").astype(jnp.float32),
        lax.psum(all_shares[5].astype(jnp.bfloat16), "seq").astype(jnp.float32),
        lax.psum(all_shares[6].astype(jnp.bfloat16), "seq").astype(jnp.float32),
        lax.psum(all_shares[7].astype(jnp.bfloat16), "seq").astype(jnp.float32),
        lax.psum(all_shares[8].astype(jnp.bfloat16), "seq").astype(jnp.float32),
        lax.psum(all_shares[9].astype(jnp.bfloat16), "seq").astype(jnp.float32),
        lax.psum(all_shares[10].astype(jnp.bfloat16), "seq").astype(jnp.float32),
        lax.psum(all_shares[11].astype(jnp.bfloat16), "seq").astype(jnp.float32),
        lax.psum(all_shares[12].astype(jnp.bfloat16), "seq").astype(jnp.float32),
    )
    return (
        output,
        grad_inputs,
        grad_first_gain,
        grad_first_shift,
        grad_qkv_weight,
        grad_query_bias,
        grad_value_bias,
        grad_out_weight,
        grad_out_bias,
        grad_second_gain,
        grad_second_shift,
        grad_fc_weight,
        grad_fc_bias,
        grad_proj_weight,
        grad_proj_bias,
    )


def solution(mesh):
    in_specs = (
        P("rows", "seq", None),
        P("rows", "seq"),
        P(),
        P(),
        P(),
        P(),
        P(),
        P(),
        P(),
        P(),
        P(),
        P(),
        P(),
        P(),
        P(),
        P("rows", "seq", None),
    )
    out_specs = (
        P("rows", "seq", None),
        P("rows", "seq", None),
        P("rows"),
        P("rows"),
        P("rows", None),
        P("rows"),
        P("rows"),
        P("rows", None),
        P("rows"),
        P("rows"),
        P("rows"),
        P("rows", None),
        P("rows"),
        P("rows", None),
        P("rows"),
    )
    return jax.shard_map(local, mesh=mesh, in_specs=in_specs, out_specs=out_specs, check_vma=False)
```

profile of v0, /device:TPU:0, one launch (start us, length us, event | category | flops | bytes accessed | tf_op | source)
XLA Modules:
  0.0 853.2 jit_solution(14614406170986299367)
XLA Ops:
  7.3 1.8 convert_reduce_fusion
  9.2 2.1 fusion.40
  11.9 4.4 add_convert_fusion
  16.3 2.1 copy-done.9
  18.5 1.9 fusion.62
  20.4 3.7 slice.49
  26.1 5.3 all_gather.12
  33.9 2.7 copy.55
  36.6 31.5 %all-gather.5.cloned.1.call-done = bf16[2,1024,768]{2,1,0:T(8,128)(2,1)} async-done(((bf16[2,512,768]{2,1,0:T(8,128)(2,1)}), bf16[2,1024,768]{2,1,0:T(8,128)(2,1)}) %all-gather.5.cloned.1.call-update) | async-done | bytes 3145744 | tf_op jit(solution)/shard_map/all_gather | solution.py:207
  68.1 54.2 %conditional.3 = (f32[2,12,512]{2,1,0:T(8,128)}, f32[2,12,512]{2,1,0:T(8,128)}) conditional(s32[]{:T(128)} %convert_element_type.180, () %tuple.41, (s32[512]{0:T(512)S(1)}, s32[2,1024]{1,0:T(2,128)S(1)}, s32[2,512]{1,0:T(2,128)S(1)}, bf16[2,1024,768]{2,1,0:T(8,128)(2,1)}, bf16[2,512,12,64]{1,3,2,0:T(8,128)(2,1)}) %tuple.105), branch_computations={%region_5.0_spmd, %region_6.9_spmd} | conditional | flops 1713885184 | bytes 116127760 | solution.py:74
  68.5 1.8 compare_and_fusion
  70.3 4.7 copy.56
  75.0 22.1 %fusion = (f32[2,12,512]{2,1,0:T(8,128)S(1)}, f32[2,12,512,1024]{3,2,1,0:T(8,128)}) fusion(pred[2,512,1024]{2,1,0:T(8,128)(4,1)} %compare_and_fusion, bf16[2,512,12,64]{1,3,2,0:T(8,128)(2,1)} %get-tuple-element.60, bf16[2,1024,12,64]{1,3,2,0:T(8,128)(2,1)} %bitcast.100), kind=kOutput, calls=%fused_computation.2 | convolution fusion | flops 1648349184 | bytes 56147968 | tf_op jit(solution)/shard_map/cond/branch_1_fun/rqhd,rkhd->rhqk/dot_general | solution.py:62
  97.7 24.7 %select_reduce_fusion = f32[2,12,512]{2,1,0:T(8,128)} fusion(f32[2,12,512,1024]{3,2,1,0:T(8,128)} %get-tuple-element.227, f32[2,12,512]{2,1,0:T(8,128)} %broadcast_maximum_fusion, pred[2,512,1024]{2,1,0:T(8,128)(4,1)} %compare_and_fusion), kind=kLoop, calls=%fused_computation | loop fusion | flops 62902272 | bytes 51478528 | tf_op jit(solution)/shard_map/cond/branch_1_fun/reduce_sum | solution.py:95
  122.3 27.7 %all-gather.3.cloned.1.call-done = bf16[2,1024,1536]{2,1,0:T(8,128)(2,1)} async-done(((bf16[2,512,1536]{2,1,0:T(8,128)(2,1)}), bf16[2,1024,1536]{2,1,0:T(8,128)(2,1)}) %all-gather.3.cloned.1.call-update) | async-done | bytes 6291472 | tf_op jit(solution)/shard_map/all_gather | solution.py:217
  150.1 43.4 %conditional.4 = (bf16[2,512,768]{1,2,0:T(8,128)(2,1)}, f32[2,512,12,64]{1,3,2,0:T(8,128)}) conditional(s32[]{:T(128)} %convert_element_type.180, () %tuple.40, (s32[512]{0:T(512)S(1)}, s32[2,1024]{1,0:T(2,128)S(1)}, s32[2,512]{1,0:T(2,128)S(1)}, bf16[2,1024,1536]{2,1,0:T(8,128)(2,1)}, bf16[2,512,12,64]{1,3,2,0:T(8,128)(2,1)}, ...), branch_computations={%region_9.10_spmd, %region_10.11_spmd} | conditional | flops 3300130816 | bytes 41007120 | solution.py:74
  150.6 1.8 compare_and_fusion.1
  152.4 8.6 %copy.57 = bf16[2,1024,1536]{1,2,0:T(8,128)(2,1)} copy(bf16[2,1024,1536]{2,1,0:T(8,128)(2,1)} %get-tuple-element.155) | data formatting | bytes 12582912 | tf_op jit(solution)/shard_map
  161.0 6.2 fusion.59
  167.2 26.3 %fusion.60 = (bf16[2,512,12,64]{1,3,2,0:T(8,128)(2,1)}, f32[2,512,12,64]{1,3,2,0:T(8,128)}) fusion(bf16[2,1024,12,64]{1,3,2,0:T(8,128)(2,1)} %bitcast.105, f32[2,12,512]{2,1,0:T(8,128)} %get-tuple-element.68, f32[2,12,512]{2,1,0:T(8,128)} %get-tuple-element.67, pred[2,512,1024]{2,1,0:T(8,128)(4,1)} %compare_and_fusion.1, ...), kind=kOutput, calls=%fused_computation.102 | convolution fusion | flops 3297509376 | bytes 13729792 | tf_op jit(solution)/shard_map/cond/branch_1_fun/rhqk,rkhd->rqhd/dot_general | solution.py:113
  193.6 4.1 fusion.64
  198.5 8.5 fusion.27
  207.0 16.9 %fusion.65 = (bf16[3072]{0:T(1024)(128)(2,1)}, bf16[2,512,3072]{2,1,0:T(8,128)(2,1)}) fusion(f32[2,512,3072]{2,1,0:T(8,128)} %fusion.27, f32[3072]{0:T(1024)S(1)} %copy-done.35, bf16[3072,768]{1,0:T(8,128)(2,1)S(1)} %bitcast.110, bf16[2,512,768]{2,1,0:T(8,128)(2,1)S(1)} %copy-done.10), kind=kOutput, calls=%fused_computation.107 | convolution fusion | flops 4903400448 | bytes 25184256 | tf_op jit(solution)/shard_map/nm,km->nk/dot_general | solution.py:34
  223.9 8.5 multiply_reduce_fusion.1
  233.7 1.4 fusion.57
  236.5 2.6 convolution_convert_fusion.1
  239.0 2.6 copy.59
  241.6 1.8 convert.10
  243.4 126.8 %conditional.5 = (bf16[2,1024,1536]{1,2,0:T(8,128)(2,1)}, bf16[2,512,768]{2,1,0:T(8,128)(2,1)}) conditional(s32[]{:T(128)} %convert_element_type.180, () %tuple.44, (s32[512]{0:T(512)S(1)}, s32[2,1024]{1,0:T(2,128)S(1)}, s32[2,512]{1,0:T(2,128)S(1)}, bf16[2,1024,1536]{2,1,0:T(8,128)(2,1)}, bf16[2,512,12,64]{1,3,2,0:T(8,128)(2,1)}, ...), branch_computations={%region_15.16_spmd, %region_16.17_spmd.clone} | conditional | flops 8196444160 | bytes 329988224 | solution.py:74
  243.6 3.4 multiply_reduce_fusion
  247.4 1.8 compare_and_fusion.2
  249.2 8.6 %copy.81 = bf16[2,1024,1536]{1,2,0:T(8,128)(2,1)} copy(bf16[2,1024,1536]{2,1,0:T(8,128)(2,1)} %get-tuple-element.176) | data formatting | bytes 12582912 | tf_op jit(solution)/shard_map
  257.8 5.4 fusion.61
  263.2 23.2 %select_divide_fusion = f32[2,12,512,1024]{3,2,1,0:T(8,128)} fusion(f32[2,12,512]{2,1,0:T(8,128)} %get-tuple-element.179, f32[2,12,512]{2,1,0:T(8,128)} %get-tuple-element.178, pred[2,512,1024]{2,1,0:T(8,128)(4,1)S(1)} %copy-done.13, bf16[2,512,12,64]{1,3,2,0:T(8,128)(2,1)S(1)} %copy-done.6, bf16[2,1024,12,64]{1,3,2,0:T(8,128)(2,1)S(1)} %bitcast.102), kind=kOutput, calls=%fused_computation.16 | convolution fusion | flops 1673527296 | bytes 56197120 | tf_op jit(solution)/shard_map/cond/branch_1_fun/rqhd,rkhd->rhqk/dot_general | solution.py:62
  286.4 19.0 %fusion.8 = bf16[2,12,1024,64]{2,3,1,0:T(8,128)(2,1)} fusion(bf16[2,512,12,64]{1,3,2,0:T(8,128)(2,1)S(1)} %copy-done.1, f32[2,12,512,1024]{3,2,1,0:T(8,128)} %select_divide_fusion), kind=kOutput, calls=%fused_computation.17 | convolution fusion | flops 1623195648 | bytes 55050240 | tf_op jit(solution)/shard_map/cond/branch_1_fun/rhqk,rqhd->rkhd/dot_general | solution.py:152
  305.4 26.7 %multiply_convert_fusion = bf16[2,12,512,1024]{3,2,1,0:T(8,128)(2,1)} fusion(f32[2,12,512,1024]{3,2,1,0:T(8,128)} %select_divide_fusion, f32[2,12,512]{2,1,0:T(8,128)} %multiply_reduce_fusion, bf16[2,512,12,64]{1,3,2,0:T(8,128)(2,1)} %get-tuple-element.180, bf16[2,1024,12,64]{1,3,2,0:T(8,128)(2,1)} %bitcast.98), kind=kOutput, calls=%fused_computation.15 | convolution fusion | flops 1660944384 | bytes 80265216 | tf_op jit(solution)/shard_map/cond/branch_1_fun/rqhd,rkhd->rhqk/dot_general | solution.py:139
  332.0 14.2 %convolution_convert_fusion = bf16[2,12,512,64]{2,3,1,0:T(8,128)(2,1)} fusion(bf16[2,12,512,1024]{3,2,1,0:T(8,128)(2,1)} %multiply_convert_fusion, bf16[2,1024,12,64]{1,3,2,0:T(8,128)(2,1)} %bitcast.103), kind=kOutput, calls=%fused_computation.23 | convolution fusion | flops 1611399168 | bytes 29884416 | tf_op jit(solution)/shard_map/cond/branch_1_fun/rhqk,rkhd->rqhd/dot_general | solution.py:145
  346.3 14.8 %fusion.66 = bf16[2,12,1024,64]{2,3,1,0:T(8,128)(2,1)} fusion(bf16[2,512,12,64]{1,3,2,0:T(8,128)(2,1)} %get-tuple-element.177, bf16[2,12,512,1024]{3,2,1,0:T(8,128)(2,1)} %multiply_convert_fusion), kind=kOutput, calls=%fused_computation.108 | convolution fusion | flops 1610612736 | bytes 29884416 | tf_op jit(solution)/shard_map/cond/branch_1_fun/rhqk,rqhd->rkhd/dot_general | solution.py:149
  361.1 2.6 copy.82
  363.7 6.2 pad_maximum_fusion
  370.3 8.6 %copy.61 = bf16[2,1024,1536]{2,1,0:T(8,128)(2,1)} copy(bf16[2,1024,1536]{1,2,0:T(8,128)(2,1)} %get-tuple-element.104) | data formatting | bytes 12582912 | tf_op jit(solution)/shard_map/cond | solution.py:74
  379.0 4.3 bitcast_convert_fusion.3
  383.3 14.0 %bitcast_convert_fusion = bf16[3072,768]{1,0:T(8,128)(2,1)} fusion(bf16[2,512,768]{2,1,0:T(8,128)(2,1)} %param.37, f32[2,512,3072]{2,1,0:T(8,128)} %fusion.27, f32[3072]{0:T(1024)S(1)} %copy-done.36), kind=kOutput, calls=%fused_computation.34 | convolution fusion | flops 4868014080 | bytes 18886656 | tf_op jit(solution)/shard_map/nk,nm->km/dot_general | solution.py:41
  398.0 10.5 %bitcast_convert_fusion.1 = bf16[768,3072]{1,0:T(8,128)(2,1)} fusion(bf16[2,512,3072]{2,1,0:T(8,128)(2,1)} %get-tuple-element.244, f32[2,512,768]{2,1,0:T(8,128)} %copy-done.7, f32[768]{0:T(1024)S(1)} %copy-done.38, f32[768]{0:T(1024)S(1)} %copy-done.31, f32[2,512]{1,0:T(2,128)S(1)} %copy-done.29, f32[2,512]{1,0:T(2,128)S(1)} %copy-done.22), kind=kOutput, calls=%fused_computation.35 | convolution fusion | flops 4838129664 | bytes 14170112 | tf_op jit(solution)/shard_map/nk,nm->km/dot_general | solution.py:41
  408.6 2.7 constant_dynamic-update-slice_fusion.1
  411.3 44.8 %reduce-scatter.6.cloned.1.call-done = bf16[2,512,1536]{2,1,0:T(8,128)(2,1)} async-done(((bf16[2,1024,1536]{2,1,0:T(8,128)(2,1)}), bf16[2,512,1536]{2,1,0:T(8,128)(2,1)}) %reduce-scatter.6.cloned.1.call-update) | async-done | bytes 3145744 | tf_op jit(solution)/shard_map/reduce_scatter | solution.py:268
  456.1 4.0 constant_dynamic-update-slice_fusion
  460.2 8.0 bitcast_convert_fusion.2
  471.0 13.6 %add_convert_fusion.2 = bf16[2,512,768]{2,1,0:T(8,128)(2,1)} fusion(f32[2,512,768]{2,1,0:T(8,128)} %copy-done.7, bf16[3072,768]{1,0:T(8,128)(2,1)} %param.35, f32[768]{0:T(1024)S(1)} %copy-done.41, f32[2,512,3072]{2,1,0:T(8,128)} %fusion.27, f32[3072]{0:T(1024)} %param.34), kind=kOutput, calls=%fused_computation.72 | convolution fusion | flops 4866441216 | bytes 22035456 | tf_op jit(solution)/shard_map/dot_general | solution.py:28
  484.6 3.6 reduce.3
  488.3 7.6 fusion.56
  495.9 1.6 copy-done.8
  497.6 2.2 fusion.38
  499.8 18.4 %reduce-scatter.10.cloned.1.call-done = bf16[48,768]{1,0:T(8,128)(2,1)} async-done(((bf16[768,768]{1,0:T(8,128)(2,1)}), bf16[48,768]{1,0:T(8,128)(2,1)}) %reduce-scatter.10.cloned.1.call-update) | async-done | bytes 73744 | tf_op jit(solution)/shard_map/reduce_scatter | solution.py:295
  518.2 78.8 %reduce-scatter.14.cloned.1.call-done = bf16[192,768]{1,0:T(8,128)(2,1)} async-done(((bf16[3072,768]{1,0:T(8,128)(2,1)}), bf16[192,768]{1,0:T(8,128)(2,1)}) %reduce-scatter.14.cloned.1.call-update) | async-done | bytes 294928 | tf_op jit(solution)/shard_map/reduce_scatter | solution.py:313
  597.0 78.3 %reduce-scatter.12.cloned.1.call-done = bf16[48,3072]{1,0:T(8,128)(2,1)} async-done(((bf16[768,3072]{1,0:T(8,128)(2,1)}), bf16[48,3072]{1,0:T(8,128)(2,1)}) %reduce-scatter.12.cloned.1.call-update) | async-done | bytes 294928 | tf_op jit(solution)/shard_map/reduce_scatter | solution.py:307
  675.3 71.5 %reduce-scatter.8.cloned.1.call-done = bf16[48,2304]{1,0:T(8,128)(2,1)} async-done(((bf16[768,2304]{1,0:T(8,128)(2,1)}), bf16[48,2304]{1,0:T(8,128)(2,1)}) %reduce-scatter.8.cloned.1.call-update) | async-done | bytes 221200 | tf_op jit(solution)/shard_map/reduce_scatter | solution.py:286
  748.2 57.7 %all-reduce.9 = (bf16[768]{0:T(1024)(128)(2,1)}, bf16[768]{0:T(1024)(128)(2,1)}, bf16[768]{0:T(1024)(128)(2,1)}, bf16[768]{0:T(1024)(128)(2,1)}, bf16[768]{0:T(1...) all-reduce(bf16[768]{0:T(1024)(128)(2,1)} %get-tuple-element.195, ...), channel_id=3, replica_groups=mesh['seq'=2,'rows'=16] {'rows'}, use_global_device_ids=true, to_apply=%region_21.22.clone | all-reduce | flops 9216 | bytes 36864
  817.0 5.6 all-reduce.10
  833.9 5.4 add_convert_fusion.1
  839.3 1.6 convert_element_type.203
  840.8 1.7 convert_element_type.198
  842.5 1.8 convert_element_type.210
  844.4 1.8 convert_element_type.213
  (150 shorter events, 35.1 us)
Async XLA Ops:
  7.2 4.7 copy-start
  7.2 4.7 copy-start.32
  7.2 4.7 copy-start.33
  7.2 4.7 copy-start.25
  7.2 4.7 copy-start.39
  7.2 60.9 %all-gather.5.cloned.1.call-start = ((), (), s32[]{:S(2)}) async-start(), calls=%async_computation.6 | async-start | bytes 4718592 | tf_op jit(solution)/shard_map/all_gather | solution.py:207
  7.3 4.6 copy-start.3
  9.1 7.2 copy-start.15
  11.3 0.6 copy-start.23
  11.3 5.0 copy-start.17
  16.3 2.1 copy-start.9
  20.3 129.7 %all-gather.3.cloned.1.call-start = ((), (), s32[]{:S(2)}) async-start(), calls=%async_computation.5 | async-start | bytes 9437184 | tf_op jit(solution)/shard_map/all_gather | solution.py:217
  24.1 0.7 copy-start.14
  24.1 432.0 %reduce-scatter.6.cloned.1.call-start = ((), (), s32[]{:S(2)}) async-start(), calls=%async_computation.7 | async-start | bytes 9437184 | tf_op jit(solution)/shard_map/reduce_scatter | solution.py:268
  193.5 4.7 slice-start
  193.5 4.8 slice-start.1
  193.5 13.5 %slice-start.2 = ((s8[4718592]{0:T(1024)(128)(4,1)}), s8[4194304]{0:T(1024)(128)(4,1)S(1)}, s32[]{:S(2)}) async-start(s8[4718592]{0:T(1024)(128)(4,1)} %bitcast.109), calls=%async_computation.15 | async-start | bytes 8388608
  197.7 34.7 %copy-start.7 = (f32[2,512,768]{2,1,0:T(8,128)}, f32[2,512,768]{2,1,0:T(8,128)S(1)}, u32[]{:S(2)}) copy-start(f32[2,512,768]{2,1,0:T(8,128)S(1)} %get-tuple-element.240) | copy-start | bytes 9437188
  197.7 0.7 copy-start.30
  197.7 0.7 copy-start.37
  197.8 34.7 %copy-start.21 = (f32[2,512]{1,0:T(2,128)}, f32[2,512]{1,0:T(2,128)S(1)}, u32[]{:S(2)}) copy-start(f32[2,512]{1,0:T(2,128)S(1)} %broadcast_multiply_fusion) | copy-start | bytes 12292
  198.5 34.0 %copy-start.28 = (f32[2,512]{1,0:T(2,128)}, f32[2,512]{1,0:T(2,128)S(1)}, u32[]{:S(2)}) copy-start(f32[2,512]{1,0:T(2,128)S(1)} %fusion.53) | copy-start | bytes 12292
  198.5 8.5 %copy-start.10 = (bf16[2,512,768]{2,1,0:T(8,128)(2,1)S(1)}, bf16[2,512,768]{2,1,0:T(8,128)(2,1)}, u32[]{:S(2)}) copy-start(bf16[2,512,768]{2,1,0:T(8,128)(2,1)} %param.37) | copy-start | bytes 4718596
  198.5 8.5 %slice-start.3 = ((s8[4718592]{0:T(1024)(128)(4,1)}), s8[524288]{0:T(1024)(128)(4,1)S(1)}, s32[]{:S(2)}) async-start(s8[4718592]{0:T(1024)(128)(4,1)} %bitcast.109), calls=%async_computation.16 | async-start | bytes 1048576
  198.5 8.5 %copy-start.35 = (f32[3072]{0:T(1024)S(1)}, f32[3072]{0:T(1024)}, u32[]{:S(2)}) copy-start(f32[3072]{0:T(1024)} %param.34) | copy-start | bytes 36868
  233.7 1.6 copy-start.2
  233.7 1.6 copy-start.19
  233.7 2.7 copy-start.34
  235.3 1.1 copy-start.12
  257.8 5.4 copy-start.6
  257.8 5.4 copy-start.13
  263.2 23.2 %copy-start.11 = (bf16[2,1024,768]{1,2,0:T(8,128)(2,1)}, bf16[2,1024,768]{1,2,0:T(8,128)(2,1)S(1)}, u32[]{:S(2)}) copy-start(bf16[2,1024,768]{1,2,0:T(8,128)(2,1)S(1)} %get-tuple-element.233) | copy-start | bytes 9437188 | tf_op jit(solution)/shard_map/cond
  263.2 23.2 %copy-start.1 = (bf16[2,512,12,64]{1,3,2,0:T(8,128)(2,1)S(1)}, bf16[2,512,12,64]{1,3,2,0:T(8,128)(2,1)}, u32[]{:S(2)}) copy-start(bf16[2,512,12,64]{1,3,2,0:T(8,128)(2,1)} %get-tuple-element.180) | copy-start | bytes 4718596 | tf_op jit(solution)/shard_map/cond
  378.9 4.4 copy-start.36
  378.9 139.2 %reduce-scatter.10.cloned.1.call-start = ((), (), s32[]{:S(2)}) async-start(), calls=%async_computation.9 | async-start | bytes 1253376 | tf_op jit(solution)/shard_map/reduce_scatter | solution.py:295
  383.3 213.7 %reduce-scatter.14.cloned.1.call-start = ((), (), s32[]{:S(2)}) async-start(), calls=%async_computation.11 | async-start | bytes 5013504 | tf_op jit(solution)/shard_map/reduce_scatter | solution.py:313
  397.3 0.7 copy-start.22
  397.3 0.7 copy-start.29
  397.3 0.7 copy-start.31
  397.3 0.7 copy-start.38
  397.4 278.0 %reduce-scatter.12.cloned.1.call-start = ((), (), s32[]{:S(2)}) async-start(), calls=%async_computation.10 | async-start | bytes 5013504 | tf_op jit(solution)/shard_map/reduce_scatter | solution.py:307
  408.6 338.3 %reduce-scatter.8.cloned.1.call-start = ((), (), s32[]{:S(2)}) async-start(), calls=%async_computation.8 | async-start | bytes 3760128 | tf_op jit(solution)/shard_map/reduce_scatter | solution.py:286
  411.3 48.9 %copy-start.16 = (f32[2,512]{1,0:T(2,128)S(1)}, f32[2,512]{1,0:T(2,128)}, u32[]{:S(2)}) copy-start(f32[2,512]{1,0:T(2,128)} %copy-done.15) | copy-start | bytes 12292
  411.3 48.9 %copy-start.18 = (f32[2,512]{1,0:T(2,128)S(1)}, f32[2,512]{1,0:T(2,128)}, u32[]{:S(2)}) copy-start(f32[2,512]{1,0:T(2,128)} %copy-done.17) | copy-start | bytes 12292
  411.3 48.9 %copy-start.26 = (f32[768]{0:T(1024)S(1)}, f32[768]{0:T(1024)}, u32[]{:S(2)}) copy-start(f32[768]{0:T(1024)} %param.24) | copy-start | bytes 9220
  411.3 48.9 %copy-start.40 = (f32[768]{0:T(1024)S(1)}, f32[768]{0:T(1024)}, u32[]{:S(2)}) copy-start(f32[768]{0:T(1024)} %param.25) | copy-start | bytes 9220
  456.1 4.1 copy-start.4
  468.2 2.8 copy-start.41
  468.2 371.1 %all-reduce.14.cloned.1.call-start = ((), (), s32[]{:S(2)}) async-start(), calls=%async_computation.12 | async-start | bytes 1769472 | tf_op jit(solution)/shard_map/psum | solution.py:337
  488.3 7.7 copy-start.24
  488.3 9.3 %copy-start.5 = (bf16[2,512,768]{2,1,0:T(8,128)(2,1)S(1)}, bf16[2,512,768]{2,1,0:T(8,128)(2,1)}, u32[]{:S(2)}) copy-start(bf16[2,512,768]{2,1,0:T(8,128)(2,1)} %param.22) | copy-start | bytes 4718596
  488.3 9.3 %copy-start.27 = (f32[768]{0:T(1024)S(1)}, f32[768]{0:T(1024)}, u32[]{:S(2)}) copy-start(f32[768]{0:T(1024)} %param.24) | copy-start | bytes 9220
  495.9 1.6 copy-start.8
  495.9 338.0 %copy-start.20 = (f32[2,512]{1,0:T(2,128)S(1)}, f32[2,512]{1,0:T(2,128)}, u32[]{:S(2)}) copy-start(f32[2,512]{1,0:T(2,128)} %copy-done.19) | copy-start | bytes 12292
Sparse Core Ops, SparseCore 0:
  20.5 47.6 all-gather.4
  69.7 80.3 all-gather.2
  379.1 77.0 reduce-scatter.5
  460.0 58.0 reduce-scatter.9
  522.4 74.5 reduce-scatter.13
  600.7 74.5 reduce-scatter.11
  679.7 67.1 reduce-scatter.7
  749.5 35.9 all-reduce.13
where the time goes:
time: 863 us; the launch traced here: 853 us
  waiting for transfers between devices  351 us (41%)
  matrix products  249 us (29%)
  local copies, waits for them, and re-layouts  83.1 us (10%)
  other arithmetic  82.3 us (10%)
  blocking collectives  68.6 us (8%)
  between operations  17.4 us (2%)
    reduce_scatter x1, waiting for transfers between devices, local(): lax.psum_scatter(grad_proj_weight.astype(jnp.bfloat16), 'rows', scatter_d...  78.8 us
    reduce_scatter x1, waiting for transfers between devices, local(): lax.psum_scatter(grad_fc_weight.astype(jnp.bfloat16), 'rows', scatter_dim...  78.3 us
    reduce_scatter x1, waiting for transfers between devices, local(): lax.psum_scatter(grad_qkv_weight.astype(jnp.bfloat16), 'rows', scatter_di...  71.5 us
    unnamed x1, blocking collectives  57.7 us
    dot_general x2, matrix products, scaled_scores(): jnp.einsum('rqhd,rkhd->rhqk', query_heads, key_heads, preferred_element_t...  45.2 us
    reduce_scatter x1, waiting for transfers between devices, local(): lax.psum_scatter(kv_grads.astype(jnp.bfloat16), 'seq', scatter_dimension=...  44.8 us
    dot_general x4, matrix products, weight_grad(): jnp.einsum('nk,nm->km', left_flat, right_flat, preferred_element_type=jnp...  36.7 us
    dot_general x4, matrix products, back_rows(): jnp.einsum('nm,km->nk', flat_rows, weight, preferred_element_type=jnp.flo...  35.6 us
  transfers between devices with their start and end apart: 8, of which 7 were waited for; matrix products, arithmetic and copies ran while one was open for 19% of the time, Pallas kernels for 0%

commit v1 on v0

--- a/solution.py
+++ b/solution.py
@@ -1,6 +1,11 @@
+import functools
+import math
+
 import jax
 import jax.numpy as jnp
 from jax import lax
+from jax.experimental import pallas as pl
+from jax.experimental.pallas import tpu as pltpu
 from jax.sharding import PartitionSpec as P
 
 H = 12
@@ -166,6 +171,177 @@
         return (grad_query, kv_grads)
 
     return guarded(update, query_pos, query_doc)
+
+
+BF = jnp.bfloat16
+F32 = jnp.float32
+NT = (((1,), (1,)), ((), ()))
+NN = (((1,), (0,)), ((), ()))
+EXP2_SCALE = 0.125 * math.log2(math.e)
+QB = 256
+
+
+def dot(left, right, dims=NN):
+    return lax.dot_general(left, right, dims, preferred_element_type=F32)
+
+
+def build_bias(doc_row, doc_col, bias):
+    tokens = bias.shape[0]
+    for i in range(tokens // QB):
+        seen = (i + 1) * QB
+        key = lax.broadcasted_iota(jnp.int32, (seen, QB), 0)
+        query = lax.broadcasted_iota(jnp.int32, (seen, QB), 1) + i * QB
+        allowed = (key <= query) & (doc_col[0:seen, 0:1] == doc_row[0:1, i * QB : seen])
+        bias[0:seen, i * QB : seen] = jnp.where(allowed, 0.0, masked_value)
+
+
+def half_mask(pair, h):
+    lane = lax.broadcasted_iota(jnp.int32, pair.shape, 1)
+    return jnp.where((lane < HD) if h == 0 else (lane >= HD), pair, jnp.zeros_like(pair))
+
+
+def attend_kernel(q_ref, k_ref, v_ref, doc_row, doc_col, o_ref, lse_ref, bias, o_turned):
+    @pl.when(pl.program_id(0) == 0)
+    def _():
+        build_bias(doc_row, doc_col, bias)
+
+    tokens = q_ref.shape[0]
+    v_turned = v_ref[...].astype(F32).T.astype(BF)
+    queries = [half_mask(q_ref[...], h) for h in range(2)]
+
+    def scores(h, i):
+        seen = (i + 1) * QB
+        here = slice(i * QB, seen)
+        return dot(k_ref[0:seen, :], queries[h][here], NT) * EXP2_SCALE + bias[0:seen, here]
+
+    jobs = [(h, i) for i in range(tokens // QB) for h in range(2)]
+    results = {}
+    now = scores(*jobs[0])
+    for place, (h, i) in enumerate(jobs):
+        later = scores(*jobs[place + 1]) if place + 1 < len(jobs) else None
+        seen = (i + 1) * QB
+        top = jnp.max(now, axis=0, keepdims=True)
+        probs = jnp.exp2(now - top)
+        mass = jnp.sum(probs, axis=0, keepdims=True)
+        part = dot(v_turned[h * HD : (h + 1) * HD, :seen], probs.astype(BF))
+        results[h, i] = (part / mass, top + jnp.log2(mass))
+        now = later
+    for (h, i), (part, lse) in results.items():
+        here = slice(i * QB, (i + 1) * QB)
+        o_turned[h * HD : (h + 1) * HD, here] = part
+        lse_ref[0, h : h + 1, here] = lse
+    o_ref[...] = o_turned[...].T.astype(BF)
+
+
+def attend(mixed, doc_row, doc_col):
+    tokens = mixed.shape[0]
+    pairs = H // 2
+    width = 2 * HD
+    part = lambda base: pl.BlockSpec((tokens, width), lambda p: (0, base + p))
+    return pl.pallas_call(
+        attend_kernel,
+        grid=(pairs,),
+        out_shape=(
+            jax.ShapeDtypeStruct((tokens, H * HD), BF),
+            jax.ShapeDtypeStruct((pairs, 2, tokens), F32),
+        ),
+        in_specs=[
+            part(0),
+            part(pairs),
+            part(2 * pairs),
+            pl.BlockSpec((1, tokens), lambda p: (0, 0)),
+            pl.BlockSpec((tokens, 1), lambda p: (0, 0)),
+        ],
+        out_specs=(part(0), pl.BlockSpec((1, 2, tokens), lambda p: (p, 0, 0))),
+        scratch_shapes=[pltpu.VMEM((tokens, tokens), F32), pltpu.VMEM((width, tokens), F32)],
+        compiler_params=pltpu.CompilerParams(vmem_limit_bytes=50 << 20),
+        cost_estimate=pl.CostEstimate(flops=3 << 30, bytes_accessed=6 << 20, transcendentals=8 << 20),
+        name="attend",
+    )(mixed, mixed, mixed, doc_row, doc_col)
+
+
+def attend_back_kernel(
+    q_ref, k_ref, v_ref, do_ref, o_ref, lse_ref, doc_row, doc_col, dq_ref, dk_ref, dv_ref, bias, dq_turned, dk, dv
+):
+    @pl.when(pl.program_id(0) == 0)
+    def _():
+        build_bias(doc_row, doc_col, bias)
+
+    tokens = q_ref.shape[0]
+    products = (do_ref[...].astype(F32) * o_ref[...].astype(F32)).T
+    k_turned = k_ref[...].astype(F32).T.astype(BF)
+    dk[...] = jnp.zeros_like(dk)
+    dv[...] = jnp.zeros_like(dv)
+    for h in range(2):
+        queries = half_mask(q_ref[...], h)
+        grads = half_mask(do_ref[...], h)
+        delta = jnp.sum(products[h * HD : (h + 1) * HD], axis=0, keepdims=True)
+        for i in range(tokens // QB):
+            seen = (i + 1) * QB
+            here = slice(i * QB, seen)
+            scores = dot(k_ref[0:seen, :], queries[here], NT) * EXP2_SCALE + bias[0:seen, here]
+            probs = jnp.exp2(scores - lse_ref[0, h : h + 1, here])
+            grad_probs = dot(v_ref[0:seen, :], grads[here], NT)
+            grad_scores = (probs * (grad_probs - delta[:, here])).astype(BF)
+            dv[0:seen, :] += dot(probs.astype(BF), grads[here])
+            dk[0:seen, :] += dot(grad_scores, queries[here])
+            dq_turned[h * HD : (h + 1) * HD, here] = dot(
+                k_turned[h * HD : (h + 1) * HD, :seen], grad_scores
+            )
+    dq_ref[...] = (dq_turned[...].T * 0.125).astype(BF)
+    dk_ref[...] = (dk[...] * 0.125).astype(BF)
+    dv_ref[...] = dv[...].astype(BF)
+
+
+def attend_back(mixed, grad_attended, attended, lse, doc_row, doc_col):
+    tokens = mixed.shape[0]
+    pairs = H // 2
+    width = 2 * HD
+    part = lambda base: pl.BlockSpec((tokens, width), lambda p: (0, base + p))
+    return pl.pallas_call(
+        attend_back_kernel,
+        grid=(pairs,),
+        out_shape=(jax.ShapeDtypeStruct((tokens, H * HD), BF),) * 3,
+        in_specs=[
+            part(0),
+            part(pairs),
+            part(2 * pairs),
+            part(0),
+            part(0),
+            pl.BlockSpec((1, 2, tokens), lambda p: (p, 0, 0)),
+            pl.BlockSpec((1, tokens), lambda p: (0, 0)),
+            pl.BlockSpec((tokens, 1), lambda p: (0, 0)),
+        ],
+        out_specs=(part(0),) * 3,
+        scratch_shapes=[
+            pltpu.VMEM((tokens, tokens), F32),
+            pltpu.VMEM((width, tokens), F32),
+            pltpu.VMEM((tokens, width), F32),
+            pltpu.VMEM((tokens, width), F32),
+        ],
+        compiler_params=pltpu.CompilerParams(vmem_limit_bytes=50 << 20),
+        cost_estimate=pl.CostEstimate(flops=12 << 30, bytes_accessed=12 << 20, transcendentals=8 << 20),
+        name="attend_back",
+    )(mixed, mixed, mixed, grad_attended, attended, lse, doc_row, doc_col)
+
+
+def swap_in(halves):
+    place = lax.axis_index("seq")
+    keep = lax.dynamic_index_in_dim(halves, place, 0, keepdims=False)
+    give = lax.dynamic_index_in_dim(halves, 1 - place, 0, keepdims=False)
+    got = lax.ppermute(give, "seq", [(0, 1), (1, 0)])
+    first = place == 0
+    return jnp.concatenate([jnp.where(first, keep, got), jnp.where(first, got, keep)], axis=0)
+
+
+def swap_out(row):
+    place = lax.axis_index("seq")
+    tokens = row.shape[0] // 2
+    keep = lax.dynamic_slice_in_dim(row, place * tokens, tokens, 0)
+    give = lax.dynamic_slice_in_dim(row, (1 - place) * tokens, tokens, 0)
+    got = lax.ppermute(give, "seq", [(0, 1), (1, 0)])
+    first = place == 0
+    return jnp.stack([jnp.where(first, keep, got), jnp.where(first, got, keep)], axis=0)
 
 
 def local(
@@ -365,6 +541,104 @@
     )
 
 
+def local_rows(
+    inputs,
+    doc_ids,
+    first_gain,
+    first_shift,
+    qkv_weight,
+    query_bias,
+    value_bias,
+    out_weight,
+    out_bias,
+    second_gain,
+    second_shift,
+    fc_weight,
+    fc_bias,
+    proj_weight,
+    proj_bias,
+    cotangent,
+):
+    branch_scale = LAYERS ** (-0.5)
+    model_width = inputs.shape[2]
+    row_docs = swap_in(doc_ids)
+    doc_row, doc_col = row_docs[None, :], row_docs[:, None]
+    residual = swap_in(inputs).astype(F32)[None]
+    normed_first, first_pull = jax.vjp(layer_norm, residual, first_gain, first_shift)
+    normed_first_low = normed_first.astype(BF)
+    bias_row = jnp.concatenate([query_bias, jnp.zeros_like(query_bias), value_bias])
+    mixed = (matmul_rows(normed_first_low, qkv_weight) + bias_row).astype(BF)[0]
+    grad_output_low = swap_in(cotangent)[None]
+    attended_low, lse = attend(mixed, doc_row, doc_col)
+    attended_low = attended_low[None]
+    middle = residual + branch_scale * (matmul_rows(attended_low, out_weight) + out_bias)
+    normed_second, second_pull = jax.vjp(layer_norm, middle, second_gain, second_shift)
+    normed_second_low = normed_second.astype(BF)
+    hidden = matmul_rows(normed_second_low, fc_weight) + fc_bias
+    activated, gelu_pull = jax.vjp(gelu_tanh, hidden)
+    activated_low = activated.astype(BF)
+    branch_two = matmul_rows(activated_low, proj_weight) + proj_bias
+    output = swap_out((middle + branch_scale * branch_two).astype(BF)[0])
+    grad_output = grad_output_low.astype(F32)
+    grad_branch_two = (branch_scale * grad_output).astype(BF)
+    grad_proj_weight = weight_grad(activated_low, grad_branch_two)
+    grad_hidden = gelu_pull(back_rows(grad_branch_two, proj_weight))[0].astype(BF)
+    grad_fc_weight = weight_grad(normed_second_low, grad_hidden)
+    grad_from_norm, grad_second_gain, grad_second_shift = second_pull(back_rows(grad_hidden, fc_weight))
+    grad_middle = grad_output + grad_from_norm
+    grad_branch_one = (branch_scale * grad_middle).astype(BF)
+    grad_out_weight = weight_grad(attended_low, grad_branch_one)
+    grad_attended = back_rows(grad_branch_one, out_weight).astype(BF)
+    grad_mixed = attend_back(mixed, grad_attended[0], attended_low[0], lse, doc_row, doc_col)
+    grad_mixed = jnp.concatenate(grad_mixed, axis=-1)[None]
+    grad_qkv_weight = weight_grad(normed_first_low, grad_mixed)
+    mixed_sums = column_sums(grad_mixed)
+    grad_from_first, grad_first_gain, grad_first_shift = first_pull(back_rows(grad_mixed, qkv_weight))
+    grad_inputs = swap_out((grad_middle + grad_from_first).astype(BF)[0])
+    rows_count = lax.axis_size("rows")
+    vectors = (
+        grad_first_gain,
+        grad_first_shift,
+        mixed_sums[:model_width],
+        mixed_sums[2 * model_width :],
+        column_sums(grad_branch_one),
+        grad_second_gain,
+        grad_second_shift,
+        column_sums(grad_branch_two),
+        column_sums(grad_hidden),
+    )
+    packed = jnp.concatenate([v.reshape(rows_count, -1) for v in vectors], axis=1)
+    matrices = (grad_qkv_weight, grad_out_weight, grad_fc_weight, grad_proj_weight, packed)
+    shares = [
+        lax.psum(lax.psum_scatter(m.astype(BF), "rows", scatter_dimension=0, tiled=True), "seq").astype(F32)
+        for m in matrices
+    ]
+    qkv_share, out_share, fc_share, proj_share, packed_share = shares
+    cuts = []
+    at = 0
+    for v in vectors:
+        count = v.shape[0] // rows_count
+        cuts.append(packed_share[0, at : at + count])
+        at += count
+    return (
+        output,
+        grad_inputs,
+        cuts[0],
+        cuts[1],
+        qkv_share,
+        cuts[2],
+        cuts[3],
+        out_share,
+        cuts[4],
+        cuts[5],
+        cuts[6],
+        fc_share,
+        cuts[8],
+        proj_share,
+        cuts[7],
+    )
+
+
 def solution(mesh):
     in_specs = (
         P("rows", "seq", None),
@@ -401,4 +675,10 @@
         P("rows", None),
         P("rows"),
     )
-    return jax.shard_map(local, mesh=mesh, in_specs=in_specs, out_specs=out_specs, check_vma=False)
+    sizes = dict(mesh.shape)
+
+    def chosen(inputs, *others):
+        whole_rows = sizes["seq"] == 2 and inputs.shape[0] == 2
+        return (local_rows if whole_rows else local)(inputs, *others)
+
+    return jax.shard_map(chosen, mesh=mesh, in_specs=in_specs, out_specs=out_specs, check_vma=False)

time: 863 us -> 467 us (0.54)
  waiting for transfers between devices: 351 us -> 145 us
  matrix products: 249 us -> 97.5 us
  other arithmetic: 82.3 us -> 33.9 us
  Pallas kernels: 0 us -> 41.8 us
  local copies, waits for them, and re-layouts: 83.1 us -> 55.4 us
    reduce_scatter x5 -> x4, waiting for transfers between devices: 292 us -> 110 us  [local_rows(): lax.psum_scatter(m.astype(BF), 'rows', scatter_dimension=0, tiled=True)]
    dot_general x7 -> x0, matrix products: 146 us -> none  [the longest x2 45.2 us: scaled_scores(): jnp.einsum('rqhd,rkhd->rhqk', query_heads, key_heads, preferred_element_t...]
    all_gather x2 -> x0, waiting for transfers between devices: 59.3 us -> none  [the longest x1 31.5 us: local(): lax.all_gather(key_values[..., :model_width], 'seq', axis=1, tiled=True)]
    pallas_call x0 -> x2, Pallas kernels: none -> 41.8 us  [the longest x1 25.2 us: attend_back(): pl.pallas_call(attend_back_kernel, grid=(pairs,), out_shape=(jax.ShapeDty...]
    psum x1, waiting for transfers between devices: 0.01 us -> 26.1 us  [local_rows(): lax.psum(lax.psum_scatter(m.astype(BF), 'rows', scatter_dimension=0, tile...]
    reduce_sum x1 -> x0, other arithmetic: 24.7 us -> none  [update(): row_mass = jnp.sum(weights, axis=-1)]
    another operation x3 -> x0, local copies, waits for them, and re-layouts: 21.9 us -> none
    slice x7 -> x2, local copies, waits for them, and re-layouts: 21.7 us -> 1.15 us  [the longest x1 0.59 us: local_rows(): mixed_sums[2 * model_width:]]
  transfers between devices with their start and end apart: 8 -> 10, of which waited for: 7 -> 4; matrix products, arithmetic and copies ran while one was open for 19% -> 25% of each run, Pallas kernels for 0% -> 9%
where the time goes in v1:
time: 467 us; the launch traced here: 460 us
  waiting for transfers between devices  145 us (31%)
  matrix products  97.5 us (21%)
  blocking collectives  64.4 us (14%)
  local copies, waits for them, and re-layouts  55.4 us (12%)
  Pallas kernels  41.8 us (9%)
  other arithmetic  33.9 us (7%)
  between operations  15 us (3%)
  starting transfers between devices  7.25 us (2%)
    reduce_scatter x4, waiting for transfers between devices, local_rows(): lax.psum_scatter(m.astype(BF), 'rows', scatter_dimension=0, tiled=True)  110 us
    unnamed x1, blocking collectives  59.5 us
    dot_general x4, matrix products, back_rows(): jnp.einsum('nm,km->nk', flat_rows, weight, preferred_element_type=jnp.flo...  40.9 us
    dot_general x4, matrix products, weight_grad(): jnp.einsum('nk,nm->km', left_flat, right_flat, preferred_element_type=jnp...  32 us
    psum x1, waiting for transfers between devices, local_rows(): lax.psum(lax.psum_scatter(m.astype(BF), 'rows', scatter_dimension=0, tile...  26.1 us
    pallas_call x1, Pallas kernels, attend_back(): pl.pallas_call(attend_back_kernel, grid=(pairs,), out_shape=(jax.ShapeDty...  25.2 us
    dot_general x4, matrix products, matmul_rows(): result = jnp.dot(flat_rows, weight, preferred_element_type=jnp.float32)  24.6 us
    unnamed x136, local copies, waits for them, and re-layouts  18.6 us
  transfers between devices with their start and end apart: 10, of which 4 were waited for; matrix products, arithmetic and copies ran while one was open for 25% of the time, Pallas kernels for 9%

profile of v1, /device:TPU:0, one launch (start us, length us, event | category | flops | bytes accessed | tf_op | source)
XLA Modules:
  0.0 460.1 jit_solution(3014623414188112496)
XLA Ops:
  7.3 3.7 constant_dynamic-slice_fusion.2
  11.0 2.3 copy.56
  13.3 3.0 collective-permute-start
  16.9 2.3 copy.60
  19.2 2.0 collective-permute-start.3
  21.9 2.3 copy.59
  24.2 2.3 copy.55
  26.5 8.5 %collective-permute-done.1 = s32[512]{0:T(512)} collective-permute-done((s32[512]{0:T(512)}, s32[512]{0:T(512)}, u32[]{:S(2)}, u32[]{:S(2)}) %collective-permute-start.1) | collective-permute-done | bytes 2080 | tf_op jit(solution)/shard_map/ppermute | solution.py:332
  35.7 1.0 copy.57.doc_col
  36.7 1.5 bitcast_select_fusion.3
  39.0 5.9 %add_convert_fusion.q_ref.k_ref.v_ref = bf16[1024,2304]{1,0:T(8,128)(2,1)} fusion(bf16[768,2304]{1,0:T(8,128)(2,1)S(1)} %copy-done, f32[2304]{0:T(1024)S(1)} %pad_maximum_fusion.5, f32[768]{0:T(1024)S(1)} %copy-done.60, f32[768]{0:T(1024)S(1)} %copy-done.52, f32[1024]{0:T(1024)S(1)} %fusion.23, f32[1024]{0:T(1024)S(1)} %broadcast_multiply_fusion.1, ...), kind=kOutput, calls=%fused_computation.10 | convolution fusion | flops 3635675136 | bytes 9853952 | tf_op jit(solution)/shard_map/dot_general | solution.py:33
  45.0 16.6 %attend.1 = (bf16[1024,768]{1,0:T(8,128)(2,1)S(1)}, f32[6,2,1024]{2,1,0:T(2,128)S(1)}) custom-call(bf16[1024,2304]{1,0:T(8,128)(2,1)} %add_convert_fusion.q_ref.k_ref.v_ref, bf16[1024,2304]{1,0:T(8,128)(2,1)} %add_convert_fusion.q_ref.k_ref.v_ref, bf16[1024,2304]{1,0:T(8,128)(2,1)} %add_convert_fusion.q_ref.k_ref.v_ref, s32[1,1024]{1,0:T(1,128)S(1)} %bitcast.64, ...), custom_call_target="tpu_custom_call" | custom-call | flops 3221225472 | bytes 6291456 | tf_op jit(solution)/shard_map/attend/pallas_call | solution.py:241
  61.7 1.7 fusion.33
  65.0 5.7 %fusion.29 = f32[1024,3072]{1,0:T(8,128)S(1)} fusion(bf16[768,3072]{1,0:T(8,128)(2,1)S(1)} %bitcast.74, f32[1024,768]{0,1:T(8,128)S(1)} %get-tuple-element.109, f32[768]{0:T(1024)S(1)} %copy-done.38, f32[768]{0:T(1024)S(1)} %copy-done.37, f32[1024]{0:T(1024)S(1)} %fusion.24, f32[1024]{0:T(1024)S(1)} %broadcast_multiply_fusion), kind=kOutput, calls=%fused_computation.96 | convolution fusion | flops 4835770368 | bytes 20461568 | tf_op jit(solution)/shard_map/dot_general | solution.py:33
  70.7 1.8 bitcast_select_fusion.1
  72.6 17.6 %fusion.36 = (bf16[3072]{0:T(1024)(128)(2,1)}, bf16[1024,3072]{1,0:T(8,128)(2,1)}) fusion(f32[1024,3072]{1,0:T(8,128)S(1)} %fusion.29, f32[3072]{0:T(1024)S(1)} %copy-done.57, bf16[3072,768]{1,0:T(8,128)(2,1)} %param.29, bf16[512,768]{0,1:T(8,128)(2,1)S(1)} %get-tuple-element.87, bf16[512,768]{0,1:T(8,128)(2,1)S(1)} %get-tuple-element.86), kind=kOutput, calls=%fused_computation.103 | convolution fusion | flops 4905759744 | bytes 25184256 | tf_op jit(solution)/shard_map/nm,km->nk/dot_general | solution.py:39
  90.2 10.5 %fusion.35 = (bf16[768]{0:T(1024)(128)(2,1)}, f32[1024,768]{1,0:T(8,128)}) fusion(bf16[1024,3072]{1,0:T(8,128)(2,1)} %get-tuple-element.115, bf16[768,3072]{1,0:T(8,128)(2,1)} %param.27), kind=kOutput, calls=%fused_computation.102 | convolution fusion | flops 4832623616 | bytes 14157312 | tf_op jit(solution)/shard_map/nm,km->nk/dot_general | solution.py:39
  100.6 3.6 copy.61
  104.3 4.5 multiply_reduce_fusion
  110.3 1.2 fusion.30
  111.6 1.1 copy-done.35
  112.7 2.5 convolution_convert_fusion.4
  115.2 4.3 convolution_convert_fusion.3.do_ref
  119.6 1.0 copy-done.6
  121.5 25.2 %attend_back.1 = (bf16[1024,768]{1,0:T(8,128)(2,1)S(1)}, bf16[1024,768]{1,0:T(8,128)(2,1)S(1)}, bf16[1024,768]{1,0:T(8,128)(2,1)}) custom-call(bf16[1024,2304]{1,0:T(8,128)(2,1)} %add_convert_fusion.q_ref.k_ref.v_ref, bf16[1024,2304]{1,0:T(8,128)(2,1)} %add_convert_fusion.q_ref.k_ref.v_ref, bf16[1024,2304]{1,0:T(8,128)(2,1)} %add_convert_fusion.q_ref.k_ref.v_ref, ...), custom_call_target="tpu_custom_call" | custom-call | flops 12884901888 | bytes 12582912 | tf_op jit(solution)/shard_map/attend_back/pallas_call | solution.py:301
  148.4 0.9 copy-done.31
  149.4 2.1 copy-done.36
  151.5 5.7 %convolution_convert_fusion.2 = bf16[768,2304]{1,0:T(8,128)(2,1)} fusion(bf16[1024,2304]{1,0:T(8,128)(2,1)S(1)} %constant_dynamic-update-slice_fusion, f32[768]{0:T(1024)S(1)} %copy-done.61, f32[768]{0:T(1024)S(1)} %copy-done.53, f32[1024]{0:T(1024)S(1)} %copy-done.44, f32[1024]{0:T(1024)S(1)} %copy-done.41, bf16[512,768]{0,1:T(8,128)(2,1)S(1)} %copy-done.19, ...), kind=kOutput, calls=%fused_computation.13 | convolution fusion | flops 3632726016 | bytes 9844736 | tf_op jit(solution)/shard_map/nk,nm->km/dot_general | solution.py:46
  157.3 13.7 %convolution_convert_fusion = bf16[3072,768]{1,0:T(8,128)(2,1)} fusion(bf16[512,768]{0,1:T(8,128)(2,1)} %copy-done.27, bf16[512,768]{0,1:T(8,128)(2,1)} %copy-done.24, f32[1024,3072]{1,0:T(8,128)} %copy-done.23, f32[3072]{0:T(1024)} %param.28), kind=kOutput, calls=%fused_computation.11 | convolution fusion | flops 4870373376 | bytes 18886656 | tf_op jit(solution)/shard_map/nk,nm->km/dot_general | solution.py:46
  171.7 10.0 %convolution_convert_fusion.1 = bf16[768,3072]{1,0:T(8,128)(2,1)} fusion(bf16[1024,3072]{1,0:T(8,128)(2,1)} %get-tuple-element.115, f32[1024,768]{0,1:T(8,128)} %copy-done.11, f32[768]{0:T(1024)S(1)} %copy-done.39, f32[768]{0:T(1024)S(1)} %copy-done.37, f32[1024]{0:T(1024)S(1)} %fusion.24, f32[1024]{0:T(1024)S(1)} %broadcast_multiply_fusion), kind=kOutput, calls=%fused_computation.12 | convolution fusion | flops 4838129664 | bytes 14170112 | tf_op jit(solution)/shard_map/nk,nm->km/dot_general | solution.py:46
  181.8 1.2 dynamic-slice.8
  183.1 11.3 %add_convert_fusion.2 = bf16[1024,768]{0,1:T(8,128)(2,1)S(1)} fusion(f32[1024,768]{0,1:T(8,128)} %copy-done.11, bf16[3072,768]{1,0:T(8,128)(2,1)} %param.29, f32[768]{0:T(1024)S(1)} %copy-done.62, f32[1024,3072]{1,0:T(8,128)} %copy-done.23, f32[3072]{0:T(1024)S(1)} %copy-done.58), kind=kOutput, calls=%fused_computation.40 | convolution fusion | flops 4866441216 | bytes 22035456 | tf_op jit(solution)/shard_map/dot_general | solution.py:33
  194.4 1.1 constant_dynamic-slice_fusion.3
  195.4 2.0 collective-permute-start.2
  197.5 8.6 %fusion.34 = (bf16[768]{0:T(1024)(128)(2,1)}, f32[1024,768]{1,0:T(8,128)}) fusion(bf16[1024,2304]{1,0:T(8,128)(2,1)} %copy-done.36, bf16[768,2304]{1,0:T(8,128)(2,1)S(1)} %copy-done), kind=kOutput, calls=%fused_computation.101 | convolution fusion | flops 3624664320 | bytes 11404800 | tf_op jit(solution)/shard_map/nm,km->nk/dot_general | solution.py:39
  206.1 3.6 copy.63
  209.7 3.5 fusion.15
  213.9 2.2 fusion.14
  216.1 1.8 add_convert_fusion.1
  217.9 1.1 constant_dynamic-slice_fusion
  219.0 0.9 maximum_reduce_fusion
  222.4 1.3 reshape.535
  223.7 1.4 reshape.534
  225.1 1.4 reshape.533
  226.5 1.4 reshape.532
  227.8 1.4 reshape.531
  229.2 1.3 reshape.530
  230.5 1.5 concatenate.83
  231.9 59.5 %all-reduce = bf16[16,576]{1,0:T(8,128)(2,1)} all-reduce(bf16[16,576]{1,0:T(8,128)(2,1)} %concatenate.83), channel_id=2, replica_groups=mesh['seq'=2,'rows'=16] {'rows'}, use_global_device_ids=true, to_apply=%region_16.17.clone | all-reduce | flops 9216 | bytes 36864
  291.4 1.4 constant_dynamic-slice_fusion.8
  292.8 4.9 %psum.35 = bf16[1,576]{1,0:T(2,128)(2,1)S(1)} all-reduce(bf16[1,576]{1,0:T(2,128)(2,1)S(1)} %constant_dynamic-slice_fusion.8), channel_id=1, replica_groups=mesh['seq'=2,'rows'=16] {'seq'}, use_global_device_ids=true, to_apply=%region_17.18 | all-reduce | flops 576 | bytes 2304 | tf_op jit(solution)/shard_map/psum | solution.py:613
  297.7 31.2 %reduce-scatter.11.cloned.1.call-done = bf16[192,768]{1,0:T(8,128)(2,1)} async-done(((bf16[3072,768]{1,0:T(8,128)(2,1)}), bf16[192,768]{1,0:T(8,128)(2,1)}) %reduce-scatter.11.cloned.1.call-update) | async-done | bytes 294928 | tf_op jit(solution)/shard_map/reduce_scatter | solution.py:613
  328.9 78.9 %reduce-scatter.9.cloned.1.call-done = bf16[48,3072]{1,0:T(8,128)(2,1)} async-done(((bf16[768,3072]{1,0:T(8,128)(2,1)}), bf16[48,3072]{1,0:T(8,128)(2,1)}) %reduce-scatter.9.cloned.1.call-update) | async-done | bytes 294928 | tf_op jit(solution)/shard_map/reduce_scatter | solution.py:613
  409.0 1.7 select_bitcast_fusion.3
  410.7 1.3 pad_maximum_fusion.2
  412.0 2.6 copy.66
  414.5 1.7 select_bitcast_fusion.1
  416.2 1.3 pad_maximum_fusion.4
  417.5 2.6 copy.67
  420.1 26.1 %all-reduce.4.cloned.1.call-done = (bf16[48,2304]{1,0:T(8,128)(2,1)}, bf16[48,768]{1,0:T(8,128)(2,1)}, bf16[48,3072]{1,0:T(8,128)(2,1)}, bf16[192,768]{1,0:T(8,128)(2,1)}) async-done(((bf16[48,2304]{1,0:T(8,128)(2,1)}, bf16[48,768]{1,0:T(8,128)(2,1)}, bf16[48,3072]{1,0:T(8,128)(2,1)}, bf16[192,768]{1,0:T(8,128)(2,1)}), (bf16[48,2304]{1,0:T(8,128)(2,1)}, bf16[48,768]{1,0:T(8,128)(2,1)}, ...) | async-done | bytes 884752 | tf_op jit(solution)/shard_map/psum | solution.py:613
  446.3 1.6 convert_element_type.167
  447.8 1.7 convert_element_type.165
  449.5 1.8 convert_element_type.169
  451.4 1.8 convert_element_type.171
  (173 shorter events, 13.7 us)
Async XLA Ops:
  7.2 31.8 %copy-start = (bf16[768,2304]{1,0:T(8,128)(2,1)S(1)}, bf16[768,2304]{1,0:T(8,128)(2,1)}, u32[]{:S(2)}) copy-start(bf16[768,2304]{1,0:T(8,128)(2,1)} %param.20) | copy-start | bytes 10616836
  7.2 290.5 %reduce-scatter.7.cloned.1.call-start = ((), (), s32[]{:S(2)}) async-start(), calls=%async_computation.5 | async-start | bytes 1253376 | tf_op jit(solution)/shard_map/reduce_scatter | solution.py:613
  7.2 9.0 %copy-start.55 = (s32[2,512]{1,0:T(2,128)S(1)}, s32[2,512]{1,0:T(2,128)}, u32[]{:S(2)}) copy-start(s32[2,512]{1,0:T(2,128)} %param.17) | copy-start | bytes 12292
  13.3 23.4 %collective-permute-start = (bf16[512,768]{0,1:T(8,128)(2,1)}, bf16[512,768]{0,1:T(8,128)(2,1)}, u32[]{:S(2)}, u32[]{:S(2)}) collective-permute-start(bf16[512,768]{0,1:T(8,128)(2,1)} %bitcast.76), channel_id=1, source_target_pairs={{0,16},{16,0},{1,17},{17,1},{2,18},{18,2},{3,19},{19,3},{4,20},{20... | collective-permute-start | bytes 2359304 | tf_op jit(solution)/shard_map/ppermute | solution.py:332
  16.8 18.1 %collective-permute-start.1 = (s32[512]{0:T(512)}, s32[512]{0:T(512)}, u32[]{:S(2)}, u32[]{:S(2)}) collective-permute-start(s32[512]{0:T(512)} %bitcast.5), channel_id=1, source_target_pairs={{0,16},{16,0},{1,17},{17,1},{2,18},{18,2},{3,19},{19,3},{4,20},{20... | collective-permute-start | bytes 6152 | tf_op jit(solution)/shard_map/ppermute | solution.py:332
  19.2 51.5 %collective-permute-start.3 = (bf16[512,768]{0,1:T(8,128)(2,1)}, bf16[512,768]{0,1:T(8,128)(2,1)}, u32[]{:S(2)}, u32[]{:S(2)}) collective-permute-start(bf16[512,768]{0,1:T(8,128)(2,1)} %bitcast.75), channel_id=1, source_target_pairs={{0,16},{16,0},{1,17},{17,1},{2,18},{18,2},{3,19},{19,3},{4,20},{20... | collective-permute-start | bytes 2359304 | tf_op jit(solution)/shard_map/ppermute | solution.py:332
  36.7 2.3 copy-start.52
  36.7 2.3 copy-start.60
  38.2 23.5 %copy-start.15 = (bf16[512,768]{0,1:T(8,128)(2,1)}, bf16[512,768]{0,1:T(8,128)(2,1)S(1)}, u32[]{:S(2)}) copy-start(bf16[512,768]{0,1:T(8,128)(2,1)S(1)} %get-tuple-element.90) | copy-start | bytes 2359300
  38.2 23.5 %copy-start.18 = (bf16[512,768]{0,1:T(8,128)(2,1)}, bf16[512,768]{0,1:T(8,128)(2,1)S(1)}, u32[]{:S(2)}) copy-start(bf16[512,768]{0,1:T(8,128)(2,1)S(1)} %get-tuple-element.91) | copy-start | bytes 2359300
  38.5 6.5 %copy-start.40 = (f32[1024]{0:T(1024)}, f32[1024]{0:T(1024)S(1)}, u32[]{:S(2)}) copy-start(f32[1024]{0:T(1024)S(1)} %broadcast_multiply_fusion.1) | copy-start | bytes 12292
  39.0 6.0 %copy-start.48 = (f32[1024]{0:T(1024)}, f32[1024]{0:T(1024)S(1)}, u32[]{:S(2)}) copy-start(f32[1024]{0:T(1024)S(1)} %fusion.17) | copy-start | bytes 12292
  39.0 6.0 %copy-start.43 = (f32[1024]{0:T(1024)}, f32[1024]{0:T(1024)S(1)}, u32[]{:S(2)}) copy-start(f32[1024]{0:T(1024)S(1)} %fusion.23) | copy-start | bytes 12292
  39.0 6.0 %copy-start.5 = (s32[1024,1]{1,0:T(8,128)S(1)}, s32[1024,1]{1,0:T(8,128)}, u32[]{:S(2)}) copy-start(s32[1024,1]{1,0:T(8,128)} %copy.57.doc_col) | copy-start | bytes 12292
  45.0 16.7 %copy-start.56 = (bf16[768,768]{1,0:T(8,128)(2,1)S(1)}, bf16[768,768]{1,0:T(8,128)(2,1)}, u32[]{:S(2)}) copy-start(bf16[768,768]{1,0:T(8,128)(2,1)} %param.23) | copy-start | bytes 3538948
  45.0 16.7 %copy-start.59 = (f32[768]{0:T(1024)S(1)}, f32[768]{0:T(1024)}, u32[]{:S(2)}) copy-start(f32[768]{0:T(1024)} %param.24) | copy-start | bytes 9220
  61.6 1.8 copy-start.7
  61.6 1.8 copy-start.9
  61.7 2.8 slice-start
  61.7 3.2 slice-start.1
  63.5 7.2 %copy-start.11 = (f32[1024,768]{0,1:T(8,128)}, f32[1024,768]{0,1:T(8,128)S(1)}, u32[]{:S(2)}) copy-start(f32[1024,768]{0,1:T(8,128)S(1)} %get-tuple-element.109) | copy-start | bytes 9437188
  63.9 6.8 %copy-start.50 = (f32[1024]{0:T(1024)}, f32[1024]{0:T(1024)S(1)}, u32[]{:S(2)}) copy-start(f32[1024]{0:T(1024)S(1)} %multiply_reduce_fusion.2) | copy-start | bytes 12292
  65.0 5.7 %copy-start.33 = (bf16[1,512,768]{1,2,0:T(8,128)(2,1)S(1)}, bf16[1,512,768]{1,2,0:T(8,128)(2,1)}, u32[]{:S(2)}) copy-start(bf16[1,512,768]{1,2,0:T(8,128)(2,1)} %copy.59) | copy-start | bytes 2359300
  70.7 19.5 %copy-start.23 = (f32[1024,3072]{1,0:T(8,128)}, f32[1024,3072]{1,0:T(8,128)S(1)}, u32[]{:S(2)}) copy-start(f32[1024,3072]{1,0:T(8,128)S(1)} %fusion.29) | copy-start | bytes 37748740
  70.7 1.9 copy-start.57
  72.6 17.6 %copy-start.24 = (bf16[512,768]{0,1:T(8,128)(2,1)}, bf16[512,768]{0,1:T(8,128)(2,1)S(1)}, u32[]{:S(2)}) copy-start(bf16[512,768]{0,1:T(8,128)(2,1)S(1)} %get-tuple-element.86) | copy-start | bytes 2359300
  72.6 17.6 %copy-start.27 = (bf16[512,768]{0,1:T(8,128)(2,1)}, bf16[512,768]{0,1:T(8,128)(2,1)S(1)}, u32[]{:S(2)}) copy-start(bf16[512,768]{0,1:T(8,128)(2,1)S(1)} %get-tuple-element.87) | copy-start | bytes 2359300
  104.2 4.5 copy-start.51
  104.3 4.5 copy-start.12
  104.3 4.7 %copy-start.14 = (f32[1024,768]{0,1:T(8,128)S(1)}, f32[1024,768]{0,1:T(8,128)}, u32[]{:S(2)}) copy-start(f32[1024,768]{0,1:T(8,128)} %copy.61) | copy-start | bytes 9437188
  109.8 1.8 copy-start.21
  109.8 1.8 copy-start.46
  110.3 2.4 copy-start.8
  119.6 178.2 %reduce-scatter.5.cloned.1.call-start = ((), (), s32[]{:S(2)}) async-start(), calls=%async_computation.4 | async-start | bytes 3760128 | tf_op jit(solution)/shard_map/reduce_scatter | solution.py:613
  146.7 1.7 copy-start.3
  146.7 2.6 copy-start.31
  146.8 4.6 %copy-start.16 = (bf16[512,768]{0,1:T(8,128)(2,1)S(1)}, bf16[512,768]{0,1:T(8,128)(2,1)}, u32[]{:S(2)}) copy-start(bf16[512,768]{0,1:T(8,128)(2,1)} %copy-done.15) | copy-start | bytes 2359300
  146.8 4.6 %copy-start.19 = (bf16[512,768]{0,1:T(8,128)(2,1)S(1)}, bf16[512,768]{0,1:T(8,128)(2,1)}, u32[]{:S(2)}) copy-start(bf16[512,768]{0,1:T(8,128)(2,1)} %copy-done.18) | copy-start | bytes 2359300
  146.8 4.6 %copy-start.41 = (f32[1024]{0:T(1024)S(1)}, f32[1024]{0:T(1024)}, u32[]{:S(2)}) copy-start(f32[1024]{0:T(1024)} %copy-done.40) | copy-start | bytes 12292
  146.9 4.6 %copy-start.44 = (f32[1024]{0:T(1024)S(1)}, f32[1024]{0:T(1024)}, u32[]{:S(2)}) copy-start(f32[1024]{0:T(1024)} %copy-done.43) | copy-start | bytes 12292
  146.9 4.6 %copy-start.53 = (f32[768]{0:T(1024)S(1)}, f32[768]{0:T(1024)}, u32[]{:S(2)}) copy-start(f32[768]{0:T(1024)} %param.18) | copy-start | bytes 9220
  146.9 4.6 %copy-start.61 = (f32[768]{0:T(1024)S(1)}, f32[768]{0:T(1024)}, u32[]{:S(2)}) copy-start(f32[768]{0:T(1024)} %param.19) | copy-start | bytes 9220
  149.4 2.1 copy-start.36
  157.2 171.7 %reduce-scatter.11.cloned.1.call-start = ((), (), s32[]{:S(2)}) async-start(), calls=%async_computation.7 | async-start | bytes 5013504 | tf_op jit(solution)/shard_map/reduce_scatter | solution.py:613
  171.0 236.8 %reduce-scatter.9.cloned.1.call-start = ((), (), s32[]{:S(2)}) async-start(), calls=%async_computation.6 | async-start | bytes 5013504 | tf_op jit(solution)/shard_map/reduce_scatter | solution.py:613
  181.8 264.5 %all-reduce.4.cloned.1.call-start = ((), (), s32[]{:S(2)}) async-start(), calls=%async_computation.8 | async-start | bytes 1769472 | tf_op jit(solution)/shard_map/psum | solution.py:613
  194.3 11.7 %copy-start.34 = (bf16[1024,768]{0,1:T(8,128)(2,1)}, bf16[1024,768]{0,1:T(8,128)(2,1)S(1)}, u32[]{:S(2)}) copy-start(bf16[1024,768]{0,1:T(8,128)(2,1)S(1)} %add_convert_fusion.2) | copy-start | bytes 4718596
  195.4 213.6 %collective-permute-start.2 = (bf16[512,768]{0,1:T(8,128)(2,1)}, bf16[512,768]{0,1:T(8,128)(2,1)}, u32[]{:S(2)}, u32[]{:S(2)}) collective-permute-start(bf16[512,768]{0,1:T(8,128)(2,1)} %constant_dynamic-slice_fusion.3), channel_id=1, source_target_pairs={{0,16},{16,0},{1,17},{17,1},{2,18},{18,2},{3,19},{19,3},{4,20},{20... | collective-permute-start | bytes 2359304 | tf_op jit(solution)/shard_map/ppermute | solution.py:342
  206.1 3.6 copy-start.42
  206.1 3.6 copy-start.54
  209.7 3.5 copy-start.49
  209.7 3.8 copy-start.13
  209.7 4.0 copy-start.17
  209.7 4.2 copy-start.20
  209.7 4.2 copy-start.45
  213.2 2.9 copy-start.22
  213.2 2.9 copy-start.26
  213.2 2.9 copy-start.29
  213.2 2.9 copy-start.47
  216.1 2.9 copy-start.2
  216.1 2.9 copy-start.4
  216.1 2.9 copy-start.32
  217.9 2.0 copy-start.30
  219.0 195.6 %collective-permute-start.4 = (bf16[512,768]{0,1:T(8,128)(2,1)}, bf16[512,768]{0,1:T(8,128)(2,1)}, u32[]{:S(2)}, u32[]{:S(2)}) collective-permute-start(bf16[512,768]{0,1:T(8,128)(2,1)} %constant_dynamic-slice_fusion), channel_id=1, source_target_pairs={{0,16},{16,0},{1,17},{17,1},{2,18},{18,2},{3,19},{19,3},{4,20},{20... | collective-permute-start | bytes 2359304 | tf_op jit(solution)/shard_map/ppermute | solution.py:342
  (11 other events, 12.9 us)
Sparse Core Ops, SparseCore 0:
  119.7 59.9 reduce-scatter.6
  183.5 67.1 reduce-scatter.4
  254.6 74.3 reduce-scatter.10
  333.1 74.6 reduce-scatter.8
  410.2 36.0 all-reduce.3
